TPU v7x, 32 devices: a whole 2x2x4 slice. The times are simulated.
32 devices in a mesh: group: 4 (over x, core), inner: 8 (over z, y).
Axes of the slice: x: 2, y: 2, z: 4, core: 2. Of those that a mesh axis runs over, the one named last changes fastest.
Arguments:
- out_grad: bfloat16 [64, 3584], P(('group', 'inner')), may hold values from -6 to 6
- routing_weight: bfloat16 [64, 4], P(('group', 'inner')), may hold values from 0.099609375 to 1
- expert_ids: int32 [64, 4], P(('group', 'inner')), may hold values from 0 to 15, as said below
- slot_index: int32 [64, 4], P(('group', 'inner')), may hold values from 0 to 5, as said below
- w_gate: bfloat16 [3584, 4096], P(None, ('group', 'inner')), may hold values from -0.09375 to 0.09375
- w_up: bfloat16 [3584, 4096], P(None, ('group', 'inner')), may hold values from -0.09375 to 0.09375
- w_down: bfloat16 [4096, 3584], P(('group', 'inner')), may hold values from -0.375 to 0.375
- pre_act: bfloat16 [2, 24, 4096], P(None, None, ('group', 'inner')), may hold values from -5 to 5
Outputs:
- grad_tokens: bfloat16 [64, 3584], P(('group', 'inner'))
- grad_routing: float32 [64, 4], P(('group', 'inner'))
Inputs may be any that keep to these rules, and one draw needn't show every extreme that they name: `expert_ids`: each token names 4 different experts, two in each of 2 different node groups (expert e lies in group e // 4). Among the 16 tokens of one index of group, every node group is named by exactly half of the tokens, and in every node group half of the experts are named by exactly 6 of these tokens and the other half by 2. slot_index[t, k] is the number of tokens before t, among the 16 tokens of the same index of group, that name expert expert_ids[t, k].
All inputs are finite; a program needn't handle non-finite values.
Results may differ from a plain program's by a relative error of at most 0.0075.
Values may be sent and summed in bfloat16 or wider, within the bound.
No kernel may reach another device: no remote copies, remote signals or barrier semaphores. Data moves between devices by JAX's collectives and lax.ppermute only.
A program may use at most 64 MiB of HBM per device.

v0:
```python
import functools

import jax
import jax.numpy as jnp
from jax import lax
from jax.experimental import pallas as pl
from jax.experimental.pallas import tpu as pltpu
from jax.sharding import Mesh, PartitionSpec as P

LANES = 128
CORES = 2
SAVED_ROWS = 32


def exchange(array, axis):
    return lax.all_to_all(array, axis, split_axis=0, concat_axis=0, tiled=True)


def pack(rows, *small):
    width = sum(s.shape[1] for s in small)
    fill = jnp.zeros((rows.shape[0], -width % LANES), rows.dtype)
    return jnp.concatenate([rows, *(s.astype(rows.dtype) for s in small), fill], axis=1)


def gradients(back_proj, weight, pre_gate, pre_up):
    gate_sig = jax.nn.sigmoid(pre_gate)
    swish_gate = pre_gate * gate_sig
    gate_piece = jnp.sum(swish_gate * pre_up * back_proj, axis=1, keepdims=True)
    scaled = weight * back_proj
    grad_up = (scaled * swish_gate).astype(jnp.bfloat16)
    grad_gate = (scaled * pre_up * gate_sig * (1.0 + pre_gate * (1.0 - gate_sig))).astype(
        jnp.bfloat16
    )
    return grad_gate, grad_up, gate_piece


def across(a, b):
    return lax.dot_general(a, b, (((1,), (1,)), ((), ())), preferred_element_type=jnp.float32)


def sizes(group_count, inner_count):
    split_count = min(8, inner_count // 4)
    return split_count, inner_count // split_count


def pack_kernel(
    out_grad, ids, slots, weights, w_gate, w_up, w_down, pre_act,
    sent, both, down, rows, words, reals, saved, small, sems,
):
    width, topk = w_gate.shape[0], ids.shape[1]
    copies = [
        pltpu.make_async_copy(source, target, sems.at[at])
        for at, (source, target) in enumerate(
            (
                (ids, words.at[0]),
                (slots, words.at[1]),
                (weights, reals),
                (out_grad, rows),
                (pre_act, saved),
                (w_gate, both.at[:width]),
                (w_up, both.at[width : 2 * width]),
                (w_down, down),
            )
        )
    ]
    for copy in copies:
        copy.start()
    small[...] = jnp.zeros_like(small)
    both[2 * width :] = jnp.zeros((both.shape[0] - 2 * width, both.shape[1]), both.dtype)
    for copy in copies[:5]:
        copy.wait()
    for at, part in enumerate((words[0], words[1], reals[...])):
        small[:, at * topk : (at + 1) * topk] = part.astype(jnp.float32)
    tail = small[...].astype(sent.dtype)
    own_rows = rows[...]
    for peer in range(sent.shape[0]):
        sent[peer, :, :width] = own_rows
        sent[peer, :, width:] = tail
    for at in range(2):
        first = 2 * width + at * SAVED_ROWS
        both[first : first + saved.shape[1]] = saved[at]
    for copy in copies[5:]:
        copy.wait()


def expert_kernel(topk, slots, arrived, both1, down1, both2, down2, out):
    half, packed = arrived.shape
    width = packed - LANES
    row_count = lax.axis_size("row")
    capacity = slots // (row_count * CORES)
    split_count, experts_here = sizes(row_count * CORES, lax.axis_size("inner"))
    core = lax.axis_index("core")
    group_row = lax.axis_index("row") * CORES
    local_expert = lax.axis_index("inner") // split_count
    small = arrived[:, width:].astype(jnp.float32)
    lane = lax.broadcasted_iota(jnp.int32, small.shape, 1)
    source = lax.broadcasted_iota(jnp.int32, (half, slots), 0) // (half // row_count)
    first = (source * CORES + core) * capacity
    column = lax.broadcasted_iota(jnp.int32, (half, slots), 1)

    def routed(group_core):
        expert = (group_row + group_core) * experts_here + local_expert
        mine = jnp.where(
            jnp.logical_and(small == expert.astype(jnp.float32), lane < topk), 1.0, 0.0
        )
        slot = jnp.sum(pltpu.roll(mine, topk, 1) * small, axis=1, keepdims=True)
        weight = jnp.sum(pltpu.roll(mine, 2 * topk, 1) * small, axis=1, keepdims=True)
        chosen = jnp.sum(mine, axis=1, keepdims=True)
        hit = jnp.logical_and(first + slot.astype(jnp.int32) == column, chosen > 0.5)
        return mine, weight, jnp.where(hit, 1.0, 0.0).astype(jnp.bfloat16)

    def backward(routing, back_proj, both):
        mine, weight, one_hot = routing
        pre_gate, pre_up = [
            jnp.dot(
                one_hot,
                both[2 * width + at * SAVED_ROWS : 2 * width + at * SAVED_ROWS + slots],
                preferred_element_type=jnp.float32,
            )
            for at in range(2)
        ]
        grad_gate, grad_up, gate_piece = gradients(back_proj, weight, pre_gate, pre_up)
        return grad_gate, grad_up, mine * gate_piece

    rows = arrived[:, :width]
    own, other = routed(core), routed(1 - core)
    grad_gate1, grad_up1, gates1 = backward(own, across(rows, down1[...]), both1)
    grad_gate2, grad_up2, gates2 = backward(other, across(rows, down2[...]), both2)
    grads = jnp.concatenate([grad_gate1, grad_up1, grad_gate2, grad_up2], axis=1)
    step = 512 if width % 512 == 0 else LANES
    for at in range(0, width, step):
        weights = [b[first + at : first + at + step] for b in (both1, both2) for first in (0, width)]
        pieces = across(grads, jnp.concatenate(weights, axis=1))
        out[:, at : at + step] = pieces.astype(out.dtype)
    out[:, width:] = (gates1 + gates2).astype(out.dtype)


def stay_in(space, *arrays):
    return [pltpu.with_memory_space_constraint(a, space) for a in arrays]


def swap_cores(array):
    return lax.ppermute(array, "core", [(0, 1), (1, 0)])


def flat(out_grad, routing_weight, expert_ids, slot_index, w_gate, w_up, w_down, pre_act):
    row_count = lax.axis_size("row")
    inner_count = lax.axis_size("inner")
    own, width = out_grad.shape
    topk = expert_ids.shape[1]
    peers = row_count * inner_count
    half = peers * own
    slots, hidden = pre_act.shape[1:]
    packed = width + LANES
    in_vmem = pl.BlockSpec(memory_space=pltpu.VMEM)
    in_hbm = pl.BlockSpec(memory_space=pltpu.HBM)
    bf16 = out_grad.dtype

    sent, both, down = pl.pallas_call(
        pack_kernel,
        out_shape=[
            jax.ShapeDtypeStruct((peers, own, packed), bf16),
            pltpu.VMEM((2 * width + 2 * SAVED_ROWS, hidden), bf16),
            pltpu.VMEM(w_down.shape, bf16),
        ],
        in_specs=[in_hbm] * 8,
        out_specs=[in_vmem] * 3,
        scratch_shapes=[
            pltpu.VMEM((own, width), bf16),
            pltpu.VMEM((2, own, topk), expert_ids.dtype),
            pltpu.VMEM((own, topk), bf16),
            pltpu.VMEM(pre_act.shape, bf16),
            pltpu.VMEM((own, LANES), jnp.float32),
            pltpu.SemaphoreType.DMA((8,)),
        ],
        compiler_params=pltpu.CompilerParams(vmem_limit_bytes=16 * 2**20),
        name="pack_rows",
    )(
        *stay_in(
            pltpu.HBM,
            *(out_grad, expert_ids, slot_index, routing_weight),
            *(w_gate, w_up, w_down, pre_act),
        )
    )
    both2, down2 = swap_cores(both), swap_cores(down)
    arrived = exchange(sent, ("row", "inner")).reshape(half, packed)
    pieces = pl.pallas_call(
        functools.partial(expert_kernel, topk, slots),
        out_shape=jax.ShapeDtypeStruct((half, packed), bf16),
        in_specs=[in_vmem] * 5,
        out_specs=in_vmem,
        compiler_params=pltpu.CompilerParams(vmem_limit_bytes=16 * 2**20),
        cost_estimate=pl.CostEstimate(
            flops=12 * half * w_down.size,
            bytes_accessed=2 * (both.nbytes + down.nbytes + arrived.nbytes),
            transcendentals=2 * half * hidden,
        ),
        name="expert_pieces",
    )(arrived, *stay_in(pltpu.VMEM, both, down, both2, down2))
    returned = exchange(pieces.reshape(peers, own, packed), ("row", "inner"))
    rows, gates = returned[:, :, :width], returned[:, :, width : width + topk]
    grad_rows = jnp.sum(rows.astype(jnp.float32), axis=0).astype(out_grad.dtype)
    return grad_rows, jnp.sum(gates.astype(jnp.float32), axis=0)


def staged(out_grad, routing_weight, expert_ids, slot_index, w_gate, w_up, w_down, pre_act):
    group_count = lax.axis_size("group")
    inner_count = lax.axis_size("inner")
    own, width = out_grad.shape
    topk = expert_ids.shape[1]
    split_count, experts_here = sizes(group_count, inner_count)
    local_expert = lax.axis_index("inner") // split_count
    block = inner_count * own
    slots = pre_act.shape[1]
    capacity = slots // group_count
    high = -(-(capacity + 1) // 8) * 8

    payload = pack(out_grad, expert_ids, slot_index, routing_weight)
    sent = jnp.broadcast_to(payload[None], (inner_count,) + payload.shape)
    arrived = exchange(sent, "inner").reshape(block, payload.shape[1])
    rows = arrived[:, :width]
    small = arrived[:, width : width + 3 * topk].astype(jnp.float32)
    ids = small[:, :topk].astype(jnp.int32)
    slot = small[:, topk : 2 * topk].astype(jnp.int32)
    weight = small[:, 2 * topk :]
    selected = ids % experts_here == local_expert
    column = ids // experts_here * high + slot
    one_hot = jnp.logical_and(
        column[:, :, None] == jnp.arange(group_count * high, dtype=jnp.int32), selected[:, :, None]
    ).astype(jnp.float32)
    placement = jnp.sum(one_hot, axis=1).astype(jnp.bfloat16)
    send_weight = jnp.sum(one_hot * weight[:, :, None], axis=(0, 1)).reshape(group_count, 1, high)
    send_rows = lax.dot_general(
        placement, rows, (((0,), (0,)), ((), ())), preferred_element_type=jnp.float32
    ).reshape(group_count, high, width)
    last = jnp.arange(high) == high - 1
    weight_row = jnp.pad(send_weight, ((0, 0), (0, 0), (0, width - high)))
    send = jnp.where(last[None, :, None], weight_row, send_rows).astype(jnp.bfloat16)
    buffer = exchange(send, "group")

    buffer_weight = buffer[:, high - 1, :capacity].astype(jnp.float32).reshape(slots, 1)
    buffer_rows = buffer[:, :capacity].reshape(slots, width)
    back_proj = across(buffer_rows, w_down)
    grad_gate, grad_up, gate_piece = gradients(
        back_proj, buffer_weight, pre_act[0].astype(jnp.float32), pre_act[1].astype(jnp.float32)
    )
    pieces = (across(grad_gate, w_gate) + across(grad_up, w_up)).reshape(group_count, capacity, width)
    gate_row = jnp.pad(
        gate_piece.reshape(group_count, 1, capacity), ((0, 0), (0, 0), (0, width - capacity))
    )
    pieces = jnp.pad(pieces, ((0, 0), (0, high - capacity), (0, 0)))
    back = exchange(jnp.where(last[None, :, None], gate_row, pieces).astype(jnp.bfloat16), "group")

    owned = jnp.dot(
        placement, back.reshape(group_count * high, width), preferred_element_type=jnp.float32
    ).astype(jnp.bfloat16)
    gates = back[:, high - 1, :high].reshape(group_count * high).astype(jnp.float32)
    gate_rows = jnp.sum(one_hot * gates, axis=2)
    final = exchange(pack(owned, gate_rows).reshape(inner_count, own, -1), "inner")
    total = jnp.sum(final.astype(jnp.float32), axis=0)
    return total[:, :width].astype(jnp.bfloat16), total[:, width : width + topk]


def solution(mesh):
    if mesh.size <= 64:
        group_count, inner_count = mesh.devices.shape
        devices = mesh.devices.reshape(group_count // CORES, CORES, inner_count)
        mesh, axes, on_device = Mesh(devices, ("row", "core", "inner")), ("row", "core", "inner"), flat
    else:
        axes, on_device = ("group", "inner"), staged
    token, hidden = P(axes, None), P(None, axes)
    return jax.shard_map(
        on_device,
        mesh=mesh,
        in_specs=(token, token, token, token, hidden, hidden, token, P(None, None, axes)),
        out_specs=(token, token),
        check_vma=False,
    )
```

profile of v0, /device:TPU:0, one launch (start us, length us, event | category | flops | bytes accessed | tf_op | source)
XLA Modules:
  0.0 38.0 jit_solution(9658579595524155266)
XLA Ops:
  0.6 1.9 %pack_rows.1 = (bf16[16,2,3712]{2,1,0:T(2,128)(2,1)S(1)}, bf16[7232,128]{1,0:T(8,128)(2,1)S(1)}, bf16[128,3584]{1,0:T(8,128)(2,1)S(1)}) custom-call(bf16[2,3584]{1,0:T(2,128)(2,1)} %out_grad.1, s32[2,4]{1,0:T(2,128)} %ids.1, s32[2,4]{1,0:T(2,128)} %slots.1, bf16[2,4]{1,0:T(2,128)(2,1)} %weights.1, bf16[3584,128]{1,0:T(8,128)(2,1)} %w_gate.1, ...), custom_call_target="tpu_custom_call" | custom-call | tf_op jit(solution)/shard_map/pack_rows/pallas_call | solution.py:159
  2.5 0.5 %collective-permute-start = (bf16[7232,128]{1,0:T(8,128)(2,1)S(1)}, bf16[7232,128]{1,0:T(8,128)(2,1)}, u32[]{:S(2)}, u32[]{:S(2)}) collective-permute-start(bf16[7232,128]{1,0:T(8,128)(2,1)S(1)} %get-tuple-element.6.both1), channel_id=1, source_target_pairs={{0,8},{8,0},{1,9},{9,1},{2,10},{10,2},{3,11},{11,3},{4,12},{12,4},... | collective-permute-start | bytes 5554184 | tf_op jit(solution)/shard_map/ppermute | solution.py:143
  3.0 0.1 collective-permute-start.1
  3.1 17.7 %all_to_all.10 = bf16[16,2,3712]{2,1,0:T(2,128)(2,1)S(1)} all-to-all(bf16[16,2,3712]{2,1,0:T(2,128)(2,1)S(1)} %get-tuple-element.5), channel_id=1, replica_groups=mesh['row'=2,'core'=2,'inner'=8] {'row','inner'}, dimensions={0} | all-to-all | bytes 475136 | tf_op jit(solution)/shard_map/all_to_all | solution.py:16
  20.9 0.1 reshape.10.arrived
  20.9 0.0 collective-permute-done.1.down2
  21.0 0.0 collective-permute-done.both2
  21.0 3.5 %expert_pieces.1 = bf16[32,3712]{1,0:T(8,128)(2,1)S(1)} custom-call(bf16[32,3712]{1,0:T(8,128)(2,1)S(1)} %reshape.10.arrived, bf16[7232,128]{1,0:T(8,128)(2,1)S(1)} %get-tuple-element.6.both1, bf16[128,3584]{1,0:T(8,128)(2,1)S(1)} %get-tuple-element.7.down1, bf16[7232,128]{1,0:T(8,128)(2,1)} %collective-permute-done.both2, ...), custom_call_target="tpu_custom_call" | custom-call | flops 176160768 | bytes 6012928 | tf_op jit(solution)/shard_map/expert_pieces/pallas_call | solution.py:187
  24.4 0.1 reshape.11
  24.5 12.0 %all_to_all.11 = bf16[16,2,3712]{2,1,0:T(2,128)(2,1)S(1)} all-to-all(bf16[16,2,3712]{2,1,0:T(2,128)(2,1)S(1)} %reshape.11), channel_id=1, replica_groups=mesh['row'=2,'core'=2,'inner'=8] {'row','inner'}, dimensions={0} | all-to-all | bytes 475136 | tf_op jit(solution)/shard_map/all_to_all | solution.py:16
  36.6 0.6 %convert_reduce_fusion = f32[2,4]{1,0:T(2,128)} fusion(bf16[16,2,3712]{2,1,0:T(2,128)(2,1)S(1)} %all_to_all.11), kind=kLoop, calls=%fused_computation.1 | loop fusion | flops 248 | bytes 288 | tf_op jit(solution)/shard_map/reduce_sum | solution.py:203
  37.2 0.8 %slice_reduce_fusion = bf16[2,3584]{1,0:T(2,128)(2,1)} fusion(bf16[16,2,3712]{2,1,0:T(2,128)(2,1)S(1)} %all_to_all.11), kind=kLoop, calls=%fused_computation | loop fusion | flops 107520 | bytes 243712 | tf_op jit(solution)/shard_map/reduce_sum | solution.py:202
Async XLA Ops:
  2.5 18.4 %collective-permute-start = (bf16[7232,128]{1,0:T(8,128)(2,1)S(1)}, bf16[7232,128]{1,0:T(8,128)(2,1)}, u32[]{:S(2)}, u32[]{:S(2)}) collective-permute-start(bf16[7232,128]{1,0:T(8,128)(2,1)S(1)} %get-tuple-element.6.both1), channel_id=1, source_target_pairs={{0,8},{8,0},{1,9},{9,1},{2,10},{10,2},{3,11},{11,3},{4,12},{12,4},... | collective-permute-start | bytes 5554184 | tf_op jit(solution)/shard_map/ppermute | solution.py:143
  3.0 17.9 %collective-permute-start.1 = (bf16[128,3584]{1,0:T(8,128)(2,1)S(1)}, bf16[128,3584]{1,0:T(8,128)(2,1)}, u32[]{:S(2)}, u32[]{:S(2)}) collective-permute-start(bf16[128,3584]{1,0:T(8,128)(2,1)S(1)} %get-tuple-element.7.down1), channel_id=1, source_target_pairs={{0,8},{8,0},{1,9},{9,1},{2,10},{10,2},{3,11},{11,3},{4,12},{12,4},... | collective-permute-start | bytes 2752520 | tf_op jit(solution)/shard_map/ppermute | solution.py:143
where the time goes:
time: 38.2 us; the launch traced here: 38 us
  blocking collectives  29.8 us (78%)
  Pallas kernels  5.35 us (14%)
  other arithmetic  1.38 us (4%)
  between operations  0.68 us (2%)
  starting transfers between devices  0.6 us (2%)
    all_to_all x2, blocking collectives, exchange(): return lax.all_to_all(array, axis, split_axis=0, concat_axis=0, tiled=True)  29.8 us
    pallas_call x1, Pallas kernels, flat(): pl.pallas_call(functools.partial(expert_kernel, topk, slots), out_shape=j...  3.46 us
    pallas_call x1, Pallas kernels, flat(): pl.pallas_call(pack_kernel, out_shape=[jax.ShapeDtypeStruct((peers, own,...  1.88 us
    reduce_sum x1, other arithmetic, flat(): grad_rows = jnp.sum(rows.astype(jnp.float32), axis=0).astype(out_grad.dtype)  0.79 us
  transfers between devices with their start and end apart: 2, of which 0 were waited for; matrix products, arithmetic and copies ran while one was open for 0% of the time, Pallas kernels for 0%

commit v1 on v0

--- a/solution.py
+++ b/solution.py
@@ -41,6 +41,10 @@
 def sizes(group_count, inner_count):
     split_count = min(8, inner_count // 4)
     return split_count, inner_count // split_count
+
+
+def block_rows(width):
+    return 512 if width % 512 == 0 else LANES
 
 
 def pack_kernel(
@@ -83,9 +87,23 @@
         copy.wait()
 
 
-def expert_kernel(topk, slots, arrived, both1, down1, both2, down2, out):
+def expert_kernel(
+    topk, slots, arrived, both1, down1, both2_hbm, down2_hbm, out, both2, down2, sems
+):
     half, packed = arrived.shape
     width = packed - LANES
+    step = block_rows(width)
+    spans = [(2 * width, 2 * SAVED_ROWS)]
+    spans += [(first + at, step) for at in range(0, width, step) for first in (0, width)]
+    copies = [pltpu.make_async_copy(down2_hbm, down2, sems.at[0])]
+    copies += [
+        pltpu.make_async_copy(
+            both2_hbm.at[first : first + rows], both2.at[first : first + rows], sems.at[1 + at]
+        )
+        for at, (first, rows) in enumerate(spans)
+    ]
+    for copy in copies:
+        copy.start()
     row_count = lax.axis_size("row")
     capacity = slots // (row_count * CORES)
     split_count, experts_here = sizes(row_count * CORES, lax.axis_size("inner"))
@@ -125,10 +143,13 @@
     rows = arrived[:, :width]
     own, other = routed(core), routed(1 - core)
     grad_gate1, grad_up1, gates1 = backward(own, across(rows, down1[...]), both1)
+    copies[0].wait()
+    copies[1].wait()
     grad_gate2, grad_up2, gates2 = backward(other, across(rows, down2[...]), both2)
     grads = jnp.concatenate([grad_gate1, grad_up1, grad_gate2, grad_up2], axis=1)
-    step = 512 if width % 512 == 0 else LANES
-    for at in range(0, width, step):
+    for number, at in enumerate(range(0, width, step)):
+        copies[2 + 2 * number].wait()
+        copies[3 + 2 * number].wait()
         weights = [b[first + at : first + at + step] for b in (both1, both2) for first in (0, width)]
         pieces = across(grads, jnp.concatenate(weights, axis=1))
         out[:, at : at + step] = pieces.astype(out.dtype)
@@ -187,8 +208,13 @@
     pieces = pl.pallas_call(
         functools.partial(expert_kernel, topk, slots),
         out_shape=jax.ShapeDtypeStruct((half, packed), bf16),
-        in_specs=[in_vmem] * 5,
+        in_specs=[in_vmem] * 3 + [in_hbm] * 2,
         out_specs=in_vmem,
+        scratch_shapes=[
+            pltpu.VMEM(both.shape, bf16),
+            pltpu.VMEM(down.shape, bf16),
+            pltpu.SemaphoreType.DMA((2 + 2 * (width // block_rows(width)),)),
+        ],
         compiler_params=pltpu.CompilerParams(vmem_limit_bytes=16 * 2**20),
         cost_estimate=pl.CostEstimate(
             flops=12 * half * w_down.size,
@@ -196,7 +222,7 @@
             transcendentals=2 * half * hidden,
         ),
         name="expert_pieces",
-    )(arrived, *stay_in(pltpu.VMEM, both, down, both2, down2))
+    )(arrived, both, down, *stay_in(pltpu.HBM, both2, down2))
     returned = exchange(pieces.reshape(peers, own, packed), ("row", "inner"))
     rows, gates = returned[:, :, :width], returned[:, :, width : width + topk]
     grad_rows = jnp.sum(rows.astype(jnp.float32), axis=0).astype(out_grad.dtype)

time: 38.2 us -> 39.1 us (1.024)
  Pallas kernels: 5.35 us -> 6.22 us
    pallas_call x1, Pallas kernels: 3.46 us -> 4.34 us  [flat(): pl.pallas_call(functools.partial(expert_kernel, topk, slots), out_shape=j...]
where the time goes in v1:
time: 39.1 us; the launch traced here: 38.8 us
  blocking collectives  29.8 us (76%)
  Pallas kernels  6.22 us (16%)
  other arithmetic  1.38 us (4%)
  between operations  0.68 us (2%)
  starting transfers between devices  0.6 us (2%)
    all_to_all x2, blocking collectives, exchange(): return lax.all_to_all(array, axis, split_axis=0, concat_axis=0, tiled=True)  29.8 us
    pallas_call x1, Pallas kernels, flat(): pl.pallas_call(functools.partial(expert_kernel, topk, slots), out_shape=j...  4.34 us
    pallas_call x1, Pallas kernels, flat(): pl.pallas_call(pack_kernel, out_shape=[jax.ShapeDtypeStruct((peers, own,...  1.88 us
    reduce_sum x1, other arithmetic, flat(): grad_rows = jnp.sum(rows.astype(jnp.float32), axis=0).astype(out_grad.dtype)  0.79 us
  transfers between devices with their start and end apart: 2, of which 0 were waited for; matrix products, arithmetic and copies ran while one was open for 0% of the time, Pallas kernels for 0%

profile of v1, /device:TPU:0, one launch (start us, length us, event | category | flops | bytes accessed | tf_op | source)
XLA Modules:
  0.0 38.8 jit_solution(13403967417746367413)
XLA Ops:
  0.6 1.9 %pack_rows.1 = (bf16[16,2,3712]{2,1,0:T(2,128)(2,1)S(1)}, bf16[7232,128]{1,0:T(8,128)(2,1)S(1)}, bf16[128,3584]{1,0:T(8,128)(2,1)S(1)}) custom-call(bf16[2,3584]{1,0:T(2,128)(2,1)} %out_grad.1, s32[2,4]{1,0:T(2,128)} %ids.1, s32[2,4]{1,0:T(2,128)} %slots.1, bf16[2,4]{1,0:T(2,128)(2,1)} %weights.1, bf16[3584,128]{1,0:T(8,128)(2,1)} %w_gate.1, ...), custom_call_target="tpu_custom_call" | custom-call | tf_op jit(solution)/shard_map/pack_rows/pallas_call | solution.py:180
  2.5 0.5 %collective-permute-start = (bf16[7232,128]{1,0:T(8,128)(2,1)S(1)}, bf16[7232,128]{1,0:T(8,128)(2,1)}, u32[]{:S(2)}, u32[]{:S(2)}) collective-permute-start(bf16[7232,128]{1,0:T(8,128)(2,1)S(1)} %get-tuple-element.6.both1), channel_id=1, source_target_pairs={{0,8},{8,0},{1,9},{9,1},{2,10},{10,2},{3,11},{11,3},{4,12},{12,4},... | collective-permute-start | bytes 5554184 | tf_op jit(solution)/shard_map/ppermute | solution.py:164
  3.0 0.1 collective-permute-start.1
  3.1 17.7 %all_to_all.10 = bf16[16,2,3712]{2,1,0:T(2,128)(2,1)S(1)} all-to-all(bf16[16,2,3712]{2,1,0:T(2,128)(2,1)S(1)} %get-tuple-element.5), channel_id=1, replica_groups=mesh['row'=2,'core'=2,'inner'=8] {'row','inner'}, dimensions={0} | all-to-all | bytes 475136 | tf_op jit(solution)/shard_map/all_to_all | solution.py:16
  20.9 0.1 reshape.10.arrived
  20.9 0.0 collective-permute-done.1.down2_hbm
  21.0 0.0 collective-permute-done.both2_hbm
  21.0 4.3 %expert_pieces.1 = bf16[32,3712]{1,0:T(8,128)(2,1)S(1)} custom-call(bf16[32,3712]{1,0:T(8,128)(2,1)S(1)} %reshape.10.arrived, bf16[7232,128]{1,0:T(8,128)(2,1)S(1)} %get-tuple-element.6.both1, bf16[128,3584]{1,0:T(8,128)(2,1)S(1)} %get-tuple-element.7.down1, bf16[7232,128]{1,0:T(8,128)(2,1)} %collective-permute-done.both2_hbm, ...), custom_call_target="tpu_custom_call" | custom-call | flops 176160768 | bytes 6012928 | tf_op jit(solution)/shard_map/expert_pieces/pallas_call | solution.py:208
  25.3 0.1 reshape.11
  25.4 12.0 %all_to_all.11 = bf16[16,2,3712]{2,1,0:T(2,128)(2,1)S(1)} all-to-all(bf16[16,2,3712]{2,1,0:T(2,128)(2,1)S(1)} %reshape.11), channel_id=1, replica_groups=mesh['row'=2,'core'=2,'inner'=8] {'row','inner'}, dimensions={0} | all-to-all | bytes 475136 | tf_op jit(solution)/shard_map/all_to_all | solution.py:16
  37.4 0.6 %convert_reduce_fusion = f32[2,4]{1,0:T(2,128)} fusion(bf16[16,2,3712]{2,1,0:T(2,128)(2,1)S(1)} %all_to_all.11), kind=kLoop, calls=%fused_computation.1 | loop fusion | flops 248 | bytes 288 | tf_op jit(solution)/shard_map/reduce_sum | solution.py:229
  38.0 0.8 %slice_reduce_fusion = bf16[2,3584]{1,0:T(2,128)(2,1)} fusion(bf16[16,2,3712]{2,1,0:T(2,128)(2,1)S(1)} %all_to_all.11), kind=kLoop, calls=%fused_computation | loop fusion | flops 107520 | bytes 243712 | tf_op jit(solution)/shard_map/reduce_sum | solution.py:228
Async XLA Ops:
  2.5 18.4 %collective-permute-start = (bf16[7232,128]{1,0:T(8,128)(2,1)S(1)}, bf16[7232,128]{1,0:T(8,128)(2,1)}, u32[]{:S(2)}, u32[]{:S(2)}) collective-permute-start(bf16[7232,128]{1,0:T(8,128)(2,1)S(1)} %get-tuple-element.6.both1), channel_id=1, source_target_pairs={{0,8},{8,0},{1,9},{9,1},{2,10},{10,2},{3,11},{11,3},{4,12},{12,4},... | collective-permute-start | bytes 5554184 | tf_op jit(solution)/shard_map/ppermute | solution.py:164
  3.0 17.9 %collective-permute-start.1 = (bf16[128,3584]{1,0:T(8,128)(2,1)S(1)}, bf16[128,3584]{1,0:T(8,128)(2,1)}, u32[]{:S(2)}, u32[]{:S(2)}) collective-permute-start(bf16[128,3584]{1,0:T(8,128)(2,1)S(1)} %get-tuple-element.7.down1), channel_id=1, source_target_pairs={{0,8},{8,0},{1,9},{9,1},{2,10},{10,2},{3,11},{11,3},{4,12},{12,4},... | collective-permute-start | bytes 2752520 | tf_op jit(solution)/shard_map/ppermute | solution.py:164
